TPU v7x, 32 devices: a whole 2x2x4 slice. The times are simulated.
32 devices in a mesh: res: 8 (over z, x), samp: 4 (over y, core).
Axes of the slice: x: 2, y: 2, z: 4, core: 2. Of those that a mesh axis runs over, the one named last changes fastest.
Arguments:
- coords_pred: float32 [16, 3, 24576], P('samp', None, 'res'), may hold values from -130 to 130
- coords_true: float32 [3, 24576], P(None, 'res'), may hold values from -55 to 55
- atom_kind: int32 [24576], P('res'), may hold values from 0 to 2
- partners: int32 [192, 5], P('res'), may hold values from 0 to 191, as said below
- noise_level: float32 [16], P('samp'), may hold values from 2 to 32
Outputs:
- copy_loss: float32 [16], P('samp')
- mean_loss: float32 [], replicated
- coord_grad: float32 [16, 3, 24576], P('samp', None, 'res')
Inputs may be any that keep to these rules, and one draw needn't show every extreme that they name: `partners`: slot 0 of tile g holds g; the other used slots hold distinct tiles g' with 0 < |g' - g| <= 2, and unused slots hold g again; the pairing is symmetric (g' is listed for g exactly when g is listed for g'); some tile uses all 5 slots.
All inputs are finite; a program needn't handle non-finite values.
Results may differ from a plain program's by a relative error of at most 0.0005.
Values sent between devices are 32-bit elements; how exact they have to be, the bound alone decides.
No kernel may reach another device: no remote copies, remote signals or barrier semaphores. Data moves between devices by JAX's collectives and lax.ppermute only.
A program may use at most 64 MiB of HBM per device.

v0:
```python
import functools

import jax
import jax.numpy as jnp
from jax import lax
from jax.experimental import pallas as pl
from jax.experimental.pallas import tpu as pltpu
from jax.sharding import PartitionSpec as P

LANES = 128
BAND = 2
SWEEPS = 20
SIGMA = 16.0
HALF_THRESHOLDS = (0.25, 0.5, 1.0, 2.0)
EPS = 0.25e-6
F32 = jnp.float32
BF16 = jnp.bfloat16


def roll(x, shift, axis=1):
    return pltpu.roll(x, shift, axis)


def two_sum(a, b):
    s = a + b
    t = s - a
    return s, (a - (s - t)) + (b - t)


def two_prod(a, b):
    def halves(x):
        t = x * 4097.0
        h = t - (t - x)
        return h, x - h

    p = a * b
    ah, al = halves(a)
    bh, bl = halves(b)
    return p, ((ah * bh - p) + ah * bl + al * bh) + al * bl


def pair_add(x, y):
    s, e = two_sum(x[0], y[0])
    return two_sum(s, e + (x[1] + y[1]))


def pair_neg(x):
    return -x[0], -x[1]


def pair_mul(x, y):
    p, e = two_prod(x[0], y[0])
    return two_sum(p, e + (x[0] * y[1] + x[1] * y[0]))


def pair_div(x, w):
    q = x[0] / w
    p, e = two_prod(q, w)
    return two_sum(q, (((x[0] - p) - e) + x[1]) / w)


def dot(a, b):
    return jnp.dot(a, b, preferred_element_type=F32)


def dot_nt(a, b):
    return lax.dot_general(a, b, (((1,), (1,)), ((), ())), preferred_element_type=F32)


def split3(x):
    a = x.astype(BF16).astype(F32)
    rest = x - a
    b = rest.astype(BF16).astype(F32)
    return a, b, (rest - b).astype(BF16).astype(F32)


def stack(a, b, axis):
    return jnp.concatenate([a, b], axis=axis)


def spread(steps, work, ticks):
    state = [0, 0]

    def tick():
        state[0] += 1
        while state[1] < len(steps) and state[1] * ticks * 3 < state[0] * len(steps) * 4:
            steps[state[1]]()
            state[1] += 1

    work(tick)
    for step in steps[state[1]:]:
        step()


class Engine:
    shared = ("v", "cut", "centre", "left", "point", "acc", "score", "count")
    work = ("true", "weight", "minus", "right", "d", "f")

    def __init__(self, copies, tiles, shared, work):
        self.copies = copies
        self.twos = copies // 2
        self.low, self.high, self.dummy = tiles, tiles + BAND, tiles + 2 * BAND
        for name, ref in zip(self.shared + self.work, (*shared, *work)):
            setattr(self, name, ref)

    @staticmethod
    def shared_shapes(tiles, copies):
        n, twos = tiles + 2 * BAND + 1, copies // 2
        return [
            jax.ShapeDtypeStruct(shape, dtype)
            for shape, dtype in (
                ((n, copies + 1, 8, LANES), F32),
                ((n, 1, LANES), F32),
                ((n, copies + 1, 8, LANES), F32),
                ((n, twos + 1, LANES, LANES), BF16),
                ((n, twos, 64, 2 * LANES), BF16),
                ((n, copies * 8, LANES), F32),
                ((copies, 8, LANES), F32),
                ((8, LANES), F32),
            )
        ]

    @staticmethod
    def work_shapes(copies, parts):
        twos = copies // 2
        return [[pltpu.VMEM((LANES, LANES), F32)] * 2] * 3 + [
            [pltpu.VMEM((parts, twos + 1, LANES, 2 * LANES), BF16)] * 2,
            [pltpu.VMEM((parts, twos + 1, LANES, 2 * LANES), F32)] * 2,
            [pltpu.VMEM((parts, twos, 2 * LANES, 2 * LANES), BF16)] * 2,
        ]

    def begin_right(self):
        pick = jnp.where(lax.broadcasted_iota(jnp.int32, (LANES, LANES), 0) == 7, 1.0, 0.0).astype(BF16)
        blank = jnp.zeros((64, LANES), BF16)
        for ref in self.right:
            for k in range(ref.shape[0]):
                for h in range(self.twos + 1):
                    ref[k, h, 64:, :LANES] = blank
                    ref[k, h, :64, LANES:] = blank
                ref[k, self.twos, :, LANES:] = pick

    def place(self, t, ref):
        blank = jnp.zeros((5, LANES), F32)
        for s in range(self.copies):
            self.v[t, s] = stack(ref[pl.ds(s, 3, stride=self.copies), :], blank, 0)
        self.v[t, self.copies] = stack(ref[3 * self.copies:3 * self.copies + 3, :], blank, 0)

    @staticmethod
    def unit(k):
        return jnp.where(lax.broadcasted_iota(jnp.int32, (8, LANES), 0) == k, 1.0, 0.0)

    def prep(self, t):
        groups = []
        for s in range(self.copies + 1):
            v = self.v[t, s]
            centre = jnp.broadcast_to(jnp.sum(v, axis=1, keepdims=True) * (1.0 / LANES), (8, LANES))
            self.centre[t, s] = centre
            y = v - centre
            norm = jnp.sum(y * y, axis=0, keepdims=True)
            x = y + (self.unit(4) + EPS * self.unit(5)) + norm * self.unit(3)
            if s == self.copies:
                x = x + self.unit(7) * self.cut[t]
            a, b, c = split3(x)
            groups.append(jnp.concatenate([a, a, b, a, b, c, b, c], axis=0))
            if s < self.copies:
                a, b, c = split3(v + self.unit(3))
                p = jnp.concatenate([a, b, c, jnp.zeros_like(a)], axis=0).astype(BF16)
                q = 32 * (s % 2)
                self.point[t, s // 2, q:q + 32, :LANES] = p
                self.point[t, s // 2, q:q + 32, LANES:] = p
        groups.append(jnp.zeros((64, LANES), F32))
        for h in range(self.twos + 1):
            self.left[t, h] = stack(groups[2 * h], groups[2 * h + 1], 0).astype(BF16).T

    def build(self, slot, k, g, j, s):
        y = self.v[j, s] - self.centre[g, s]
        norm = jnp.sum(y * y, axis=0, keepdims=True)
        a, b, c = split3((self.unit(3) + self.unit(5)) - 2.0 * y + norm * self.unit(4))
        q, m = 64 * (s % 2), LANES * (s % 2)
        self.right[slot][k, s // 2, q:q + 64, m:m + LANES] = jnp.concatenate([a, b, a, c, b, a, c, b], axis=0).astype(BF16)

    def squares(self, slot, k, g, h):
        return dot(self.left[g, h], self.right[slot][k, h])

    def get(self, slot, h, k, lanes, shared):
        one = self.d[slot][0, h, k, lanes]
        if not shared:
            return one
        return jnp.where(self.upper(k), one, self.d[slot][1, h, k, lanes])

    @staticmethod
    def upper(k):
        shape = (k.stop - k.start, LANES)
        return lax.broadcasted_iota(jnp.int32, shape, 1) > lax.broadcasted_iota(jnp.int32, shape, 0) + k.start

    def weigh(self, slot, cuts, share, shared, tick):
        total = jnp.zeros((8, LANES), F32)
        for b in range(16):
            k = slice(8 * b, 8 * b + 8)
            d2 = jnp.maximum(self.get(slot, self.twos, k, slice(0, LANES), shared), EPS)
            dist = d2 * lax.rsqrt(d2)
            cut_j = jnp.where(self.upper(k), cuts[0], cuts[1]) if shared else cuts[0]
            cut_i = self.get(slot, self.twos, k, slice(LANES, 2 * LANES), shared)
            w = jnp.where(dist < cut_j, 0.0625, 0.0) + jnp.where(dist < cut_i, 0.0625, 0.0)
            if shared:
                row = lax.broadcasted_iota(jnp.int32, (8, LANES), 0) + 8 * b
                w = jnp.where(lax.broadcasted_iota(jnp.int32, (8, LANES), 1) == row, 0.0, w)
            self.true[slot][k, :] = dist
            self.weight[slot][k, :] = w
            self.minus[slot][k, :] = -w
            total = total + w
            tick()
        self.count[...] += total * share

    def factor(self, slot, share, shared, tick):
        for s in range(self.copies):
            h, m = s // 2, LANES * (s % 2)
            score = jnp.zeros((8, LANES), F32)
            blocks = []
            for q in range(8):
                k = slice(16 * q, 16 * q + 16)
                d2 = jnp.maximum(self.get(slot, h, k, slice(m, m + LANES), shared), EPS)
                r = lax.rsqrt(d2)
                diff = d2 * r - self.true[slot][k, :]
                spread = jnp.abs(diff)
                u = [jnp.tanh(t - spread) for t in HALF_THRESHOLDS]
                w = self.weight[slot][k, :]
                z = w * ((u[0] + u[1]) + (u[2] + u[3]))
                score = score + z[:8] + z[8:]
                slope = ((u[0] * u[0] + u[1] * u[1]) + (u[2] * u[2] + u[3] * u[3])) - 4.0
                f = slope * r * jnp.maximum(jnp.minimum(diff * 1e30, w), self.minus[slot][k, :])
                high = f.astype(BF16)
                low = (f - high.astype(F32)).astype(BF16)
                if shared:
                    blocks.append((high, low))
                else:
                    self.f[slot][0, h, k, m:m + LANES] = high
                    self.f[slot][0, h, LANES + 16 * q:LANES + 16 * q + 16, m:m + LANES] = low
                tick()
            for part, rows in enumerate(zip(*blocks)):
                whole = jnp.concatenate(rows, axis=0)
                mirror = whole.T
                for q in range(8):
                    k = slice(16 * q, 16 * q + 16)
                    upper = self.tri[0, k, :] > 0
                    start = LANES * part + 16 * q
                    self.f[slot][0, h, start:start + 16, m:m + LANES] = jnp.where(upper, whole[k], mirror[k])
                    self.f[slot][1, h, start:start + 16, m:m + LANES] = jnp.where(upper, mirror[k], whole[k])
            self.score[s] += score * share

    @staticmethod
    def fold(z):
        return [z[k:k + 8, m:m + LANES] + z[k + 8:k + 16, m:m + LANES] + z[k + 16:k + 24, m:m + LANES] for k, m in ((0, 0), (32, LANES))]

    def along_j(self, p, f):
        return self.fold(dot(p, f))

    def along_i(self, p, f):
        one = stack(f[:LANES, :LANES], f[LANES:, :LANES], 1)
        two = stack(f[:LANES, LANES:], f[LANES:, LANES:], 1)
        return self.fold(dot_nt(p, stack(one, two, 0)))

    def cross_build(self, item, slot):
        return [functools.partial(self.build, slot, 0, item[0], item[1], s) for s in range(self.copies + 1)]

    def cross_measure(self, item, slot):
        def step(h):
            self.d[slot][0, h] = self.squares(slot, 0, item[0], h)

        return [functools.partial(step, h) for h in [self.twos, *range(self.twos)]]

    def cross_factor(self, item, slot, tick):
        share = item[2].astype(F32) * 0.5
        self.weigh(slot, [self.cut[item[1]]], share, False, tick)
        self.factor(slot, share, False, tick)

    def add(self, t, h, parts):
        for q in range(2):
            self.acc[t, 8 * (2 * h + q):8 * (2 * h + q) + 8, :] += parts[q]

    def put(self, t, h, parts):
        for q in range(2):
            self.acc[t, 8 * (2 * h + q):8 * (2 * h + q) + 8, :] = parts[q]

    def cross_collect(self, item, slot):
        steps = []
        for h in range(self.twos):
            steps.append(lambda h=h: self.add(item[1], h, self.along_j(self.point[item[0], h], self.f[slot][0, h])))
            steps.append(lambda h=h: self.add(item[0], h, self.along_i(self.point[item[1], h], self.f[slot][0, h])))
        return steps

    def self_build(self, item, slot):
        return [functools.partial(self.build, slot, k, item[k], item[k], s) for s in range(self.copies + 1) for k in range(2)]

    def self_measure(self, item, slot):
        def step(h, k):
            self.d[slot][k, h] = self.squares(slot, k, item[k], h)

        return [functools.partial(step, h, k) for h in [self.twos, *range(self.twos)] for k in range(2)]

    def self_factor(self, item, slot, tick):
        self.weigh(slot, [self.cut[item[0]], self.cut[item[1]]], 1.0, True, tick)
        self.factor(slot, 1.0, True, tick)

    def self_collect(self, item, slot):
        steps = []
        for h in range(self.twos):
            for k in range(2):
                steps.append(lambda h=h, k=k: self.put(item[k], h, self.along_j(self.point[item[k], h], self.f[slot][k, h])))
        return steps

    def half(self, kind, items, slot):
        last, now, soon, later = items
        steps = getattr(self, kind + "_collect")(last, 1 - slot)
        steps += getattr(self, kind + "_measure")(soon, 1 - slot)
        steps += getattr(self, kind + "_build")(later, 1 - slot)
        spread(steps, lambda tick: getattr(self, kind + "_factor")(now, slot, tick), 16 + 8 * self.copies)

    def begin_list(self, kind, item, n):
        steps = getattr(self, kind + "_build")(item(0), 0)
        steps += getattr(self, kind + "_measure")(item(0), 0)
        for i in (1, 2):
            steps += getattr(self, kind + "_build")(item(jnp.minimum(i, n - 1)), i % 2)
        for step in steps:
            step()

    def run_list(self, kind, item, n, dummy):
        def at(p):
            return tuple(jnp.where(p < 0, dummy, z) for z in item(jnp.clip(p, 0, n - 1)))

        @pl.loop(0, n // 2)
        def _(i):
            p = 2 * i
            for slot in range(2):
                self.half(kind, [at(p + slot - 1), at(p + slot), at(p + slot + 1), at(p + slot + 3)], slot)

    def end_list(self, kind, item, n, dummy):
        def last(i, slot):
            return getattr(self, kind + "_collect")(item(i), slot)

        def odd():
            before = tuple(jnp.where(n > 1, z, dummy) for z in item(jnp.maximum(n - 2, 0)))
            steps = getattr(self, kind + "_collect")(before, 1)
            spread(steps, lambda tick: getattr(self, kind + "_factor")(item(n - 1), 0, tick), 16 + 8 * self.copies)
            for step in last(n - 1, 0):
                step()

        def even():
            for step in last(n - 1, 1):
                step()

        if isinstance(n, int):
            (odd if n % 2 else even)()
        else:
            pl.when(n % 2 == 1)(odd)
            pl.when(n % 2 == 0)(even)

    def scores(self, weight_total):
        rows = [jnp.sum(self.score[s], axis=0, keepdims=True) for s in range(self.copies)]
        rows += [jnp.sum(self.count[...], axis=0, keepdims=True), weight_total]
        total = jnp.zeros((8, LANES), F32)
        for k, x in enumerate(rows):
            total = total + x * self.unit(2 + k)
        return jnp.broadcast_to(jnp.sum(total, axis=1, keepdims=True), (8, LANES))


def self_kernel(base_ref, part_ref, pred_ref, true_ref, kind_ref, *refs, copies, tiles):
    count = len(Engine.shared)
    shared, (items, moment_ref), (x_ref, sum_ref, tri), work = refs[:count], refs[count:count + 2], refs[count + 2:count + 5], refs[count + 5:]
    e = Engine(copies, tiles, shared, work)
    e.tri = tri
    base = base_ref[0]
    rows = 3 * copies
    e.begin_right()
    for ref in [e.score, e.count, x_ref, sum_ref, *(r.at[e.dummy] for r in shared[:5])]:
        ref[...] = jnp.zeros_like(ref)
    row = lax.broadcasted_iota(jnp.int32, (LANES, LANES), 0)
    lane = lax.broadcasted_iota(jnp.int32, (LANES, LANES), 1)
    tri[0] = jnp.where(lane > row, 1.0, 0.0).astype(BF16)

    place = lax.broadcasted_iota(jnp.int32, (1, LANES), 1)

    def append(state, hit, g, j, share):
        n, row = state
        return n + hit, jnp.where(place == n, (share * 256 + g) * 256 + j, row)

    def partner_bits(t):
        bits = 0
        for k in range(1, part_ref.shape[0]):
            bits = bits | lax.shift_left(jnp.int32(1), (part_ref[k, t] - base) - (t - BAND))
        return lambda offset: lax.shift_right_logical(bits, BAND + offset) & 1

    unroll = next(u for u in (6, 4, 3, 2, 1) if tiles % u == 0)

    @pl.loop(0, tiles // unroll)
    def _(m):
        for q in range(unroll):
            t = m * unroll + q
            sl = pl.ds(pl.multiple_of(t * LANES, LANES), LANES)
            kind = kind_ref[:, sl]
            weight = jnp.where(kind == 1, 5.0, jnp.where(kind == 2, 10.0, 1.0))
            for c in range(3):
                x_ref[q, c * copies:(c + 1) * copies, :] = pred_ref[c, :, sl] * 0.5
            x_ref[q, rows:rows + 3, :] = true_ref[:, sl] * 0.5
            e.place(t, x_ref.at[q])
            e.cut[t] = jnp.where(kind == 1, 15.0, 7.5)
            x = x_ref[q]
            wx = x * weight
            terms = [wx * x[rows + c:rows + c + 1] for c in range(3)] + [wx, wx * x]
            for i, term in enumerate(terms):
                total, error = two_sum(sum_ref[0, i], term)
                sum_ref[0, i] = total
                sum_ref[1, i] += error
            sum_ref[0, 5, 0:1, :] += weight
            e.prep(t)

    blank = jnp.zeros((LANES - 80, LANES), F32)
    high, low = (jnp.concatenate([sum_ref[part, i] for i in range(5)] + [blank], axis=0).T for part in range(2))
    sums = [(high[8 * k:8 * k + 8], low[8 * k:8 * k + 8]) for k in range(16)]
    while len(sums) > 1:
        sums = [pair_add(a, b) for a, b in zip(sums[::2], sums[1::2])]
    sums = sums[0]
    for k in (4, 2, 1):
        sums = pair_add(sums, (roll(sums[0], k, 0), roll(sums[1], k, 0)))
    for part in range(2):
        moment_ref[part] = sums[part] * e.unit(0)
    moment_ref[2] = jnp.broadcast_to(sum_ref[0, 5, 0:1, :], (8, LANES))

    def twin(i):
        return 2 * i, 2 * i + 1

    half = tiles // 2
    e.begin_list("self", twin, half)
    e.run_list("self", twin, half, e.dummy)

    state = jnp.int32(0), jnp.zeros((1, LANES), jnp.int32)
    edges = []
    for t in range(tiles):
        bits = partner_bits(t)
        for o in range(1, BAND + 1):
            if t >= o:
                state = append(state, bits(-o), t - o, t, 2)
            else:
                edges.append((bits(-o), e.low + BAND + t - o, t, 1))
            if t + o >= tiles:
                edges.append((bits(o), t, e.high + t + o - tiles, 1))
    for edge in edges:
        state = append(state, *edge)
    n, row = state
    row = jnp.where((place == 0) & (n == 0), e.dummy * 257, row)
    items[...] = jnp.where(place == LANES - 1, jnp.maximum(n, 1), row)
    e.end_list("self", twin, half, e.dummy)


def cross_kernel(items, moment_ref, low_ref, high_ref, *refs, copies, tiles):
    count = len(Engine.shared)
    stat_ref, shared, x_ref, work = refs[count], refs[count + 1:2 * count + 1], refs[2 * count + 1], refs[2 * count + 2:]
    e = Engine(copies, tiles, shared, work)
    rows = 3 * copies
    e.begin_right()

    def item(i):
        word = items[0, i]
        return lax.shift_right_logical(word, 8) & 255, word & 255, lax.shift_right_logical(word, 16)

    n = items[0, LANES - 1]
    e.begin_list("cross", item, n)
    for i, (ref, start) in enumerate(((low_ref, e.low), (high_ref, e.high))):
        for q in range(BAND):
            t = start + q
            x_ref[BAND * i + q] = ref[:, q * LANES:(q + 1) * LANES]
            e.place(t, x_ref.at[BAND * i + q])
            e.cut[t] = x_ref[BAND * i + q, rows + 3:rows + 4, :]
            e.prep(t)
    e.run_list("cross", item, n, e.dummy)
    e.end_list("cross", item, n, e.dummy)
    stat_ref[0] = moment_ref[0] + e.scores(moment_ref[2, 0:1, :])
    stat_ref[1] = moment_ref[1]


def solve_kernel(stat_ref, other_ref, noise_ref, loss_ref, sum_ref, m_ref, k_ref, s_ref, *, copies, atoms):
    rows = 3 * copies
    stats, error = two_sum(stat_ref[0], other_ref[0])
    low = (stat_ref[1] + other_ref[1]) + error
    for part, x in enumerate((stats, low)):
        s_ref[part] = jnp.broadcast_to(x[0:1], (LANES, LANES)).T

    def per_copy(c, q, scale):
        return tuple(s_ref[part, 16 * q + c * copies:16 * q + (c + 1) * copies, :] * scale for part in range(2))

    def shared(r, q, scale):
        return tuple(s_ref[part, 16 * q + r:16 * q + r + 1, :] * scale for part in range(2))

    def wide(x):
        return tuple(jnp.broadcast_to(v, (copies, LANES)) for v in x)

    weight_sum = jnp.broadcast_to(stats[copies + 3:copies + 4], (copies, LANES))
    count = jnp.broadcast_to(stats[copies + 2:copies + 3], (copies, LANES)) * 16.0
    score = stats[2:copies + 2] * 2.0 + 0.5 * count
    pred_sum = [wide(per_copy(c, 3, 2.0)) for c in range(3)]
    true_sum = [wide(shared(rows + c, 3, 2.0)) for c in range(3)]
    pred_mean = [pair_div(x, weight_sum) for x in pred_sum]
    true_mean = [pair_div(x, weight_sum) for x in true_sum]
    cov = [[pair_add(wide(per_copy(c, d, 4.0)), pair_neg(pair_mul(pred_sum[c], true_mean[d]))) for d in range(3)] for c in range(3)]
    ct = {}
    for d in range(3):
        for e in range(d + 1):
            ct[d, e] = pair_add(wide(shared(rows + d, e, 4.0)), pair_neg(pair_mul(true_sum[d], true_mean[e])))
    var = None
    for c in range(3):
        term = pair_add(wide(per_copy(c, 4, 4.0)), pair_neg(pair_mul(pred_sum[c], pred_mean[c])))
        var = term if var is None else pair_add(var, term)

    x = [[cov[c][d][0] for d in range(3)] for c in range(3)]
    frobenius = jnp.sqrt(sum(x[c][d] * x[c][d] for c in range(3) for d in range(3)))
    x = [[x[c][d] / frobenius for d in range(3)] for c in range(3)]

    def sweep(_, flat):
        x = [flat[0:3], flat[3:6], flat[6:9]]
        gram = {}
        for a in range(3):
            for b in range(a + 1):
                gram[a, b] = gram[b, a] = x[a][0] * x[b][0] + x[a][1] * x[b][1] + x[a][2] * x[b][2]
        for a in range(3):
            for b in range(a + 1):
                gram[a, b] = gram[b, a] = (1.5 if a == b else 0.0) - 0.5 * gram[a, b]
        return tuple(gram[a, 0] * x[0][d] + gram[a, 1] * x[1][d] + gram[a, 2] * x[2][d] for a in range(3) for d in range(3))

    flat = lax.fori_loop(0, SWEEPS, sweep, tuple(v for line in x for v in line), unroll=True)
    x = [flat[0:3], flat[3:6], flat[6:9]]

    square = var
    nothing = jnp.zeros((copies, LANES), F32)
    for c in range(3):
        for d in range(3):
            square = pair_add(square, pair_mul((-2.0 * x[c][d], nothing), cov[c][d]))
    for d in range(3):
        for e in range(d + 1):
            gram = None
            for c in range(3):
                term = two_prod(x[c][d], x[c][e])
                gram = term if gram is None else pair_add(gram, term)
            if d != e:
                gram = (2.0 * gram[0], 2.0 * gram[1])
            square = pair_add(square, pair_mul(gram, ct[d, e]))

    noise = noise_ref[...]
    loss_weight = (noise * noise + SIGMA * SIGMA) / (noise * SIGMA * (noise * SIGMA))
    mean_square = (square[0] + square[1]) / (3.0 * weight_sum)
    loss = loss_weight * mean_square + 1.0 - score / count
    for s in range(copies):
        loss_ref[s] = loss[s, 0]
    sum_ref[...] = jnp.broadcast_to(jnp.sum(loss, axis=0, keepdims=True), (8, LANES))

    grad_scale = 16.0 * atoms
    for c in range(3):
        for d in range(3):
            m_ref[3 * c + d] = x[c][d]
        m_ref[9 + c] = pred_mean[c][0]
        k_ref[c:c + 1, :] = true_mean[c][0][0:1]
    m_ref[12] = grad_scale * 2.0 * loss_weight / (3.0 * weight_sum)
    m_ref[13] = grad_scale / count


def gradient_kernel(m_ref, k_ref, pred_ref, true_ref, kind_ref, acc_ref, grad_ref, *, copies, tiles):
    for t in range(tiles):
        sl = slice(t * LANES, (t + 1) * LANES)
        kind = kind_ref[:, sl]
        weight = jnp.where(kind == 1, 5.0, jnp.where(kind == 2, 10.0, 1.0))
        centred = true_ref[:, sl] - k_ref[0:3, :]
        factor_sum = 0.5 * acc_ref[t, pl.ds(3, copies, stride=8), :]
        for c in range(3):
            target = m_ref[3 * c] * centred[0:1] + m_ref[3 * c + 1] * centred[1:2] + m_ref[3 * c + 2] * centred[2:3] + m_ref[9 + c]
            pred = pred_ref[c, :, sl]
            pull = pred * factor_sum - acc_ref[t, pl.ds(c, copies, stride=8), :]
            grad_ref[c, :, sl] = m_ref[12] * weight * (pred - target) - m_ref[13] * pull


def pack_kernel(pred_hbm, true_hbm, kind_hbm, part_hbm, noise_hbm, first_ref, last_ref, pred_ref, true_ref, kind_ref, part_ref, noise_ref, noise_smem, sems, *, copies, tiles):
    span = BAND * LANES
    moves = [
        pltpu.make_async_copy(source, target, sems.at[i])
        for i, (source, target) in enumerate(
            ((pred_hbm, pred_ref), (true_hbm, true_ref), (kind_hbm, kind_ref), (part_hbm, part_ref), (noise_hbm, noise_smem))
        )
    ]
    for move in moves:
        move.start()
    for move in moves:
        move.wait()
    for ref, start in ((first_ref, 0), (last_ref, tiles * LANES - span)):
        sl = slice(start, start + span)
        for c in range(3):
            ref[c * copies:(c + 1) * copies, :] = pred_ref[c, :, sl] * 0.5
        ref[3 * copies:3 * copies + 3, :] = true_ref[:, sl] * 0.5
        ref[3 * copies + 3:3 * copies + 4, :] = jnp.where(kind_ref[:, sl] == 1, 15.0, 7.5)
    row = lax.broadcasted_iota(jnp.int32, (copies, LANES), 0)
    noise = jnp.zeros((copies, LANES), F32)
    for s in range(copies):
        noise = jnp.where(row == s, noise_smem[s], noise)
    noise_ref[...] = noise


VMEM = pl.BlockSpec(memory_space=pltpu.VMEM)
SMEM = pl.BlockSpec(memory_space=pltpu.SMEM)
PARAMS = pltpu.CompilerParams(vmem_limit_bytes=40 * 2**20)
SMALL = pltpu.CompilerParams(vmem_limit_bytes=4 * 2**20)


def swap(x, axis, step):
    return lax.ppermute(x, axis, [(i, i ^ step) for i in range(lax.axis_size(axis))])


def shards(coords_pred, coords_true, atom_kind, partners, noise_level):
    copies, _, local = coords_pred.shape
    tiles = partners.shape[0]
    rows = 3 * copies
    size = lax.axis_size("res")
    kind = atom_kind[None]
    coords_pred = jnp.transpose(coords_pred, (1, 0, 2))
    partners = partners.T
    base = (lax.axis_index("res") * tiles)[None].astype(jnp.int32)
    stats_shape = jax.ShapeDtypeStruct((2, 8, LANES), F32)

    block = jax.ShapeDtypeStruct((rows + 4, BAND * LANES), F32)
    same = [jax.ShapeDtypeStruct(x.shape, x.dtype) for x in (coords_pred, coords_true, kind, partners)]
    first, last, coords_pred, coords_true, kind, partners, noise = pl.pallas_call(
        functools.partial(pack_kernel, copies=copies, tiles=tiles),
        in_specs=[pl.BlockSpec(memory_space=pltpu.HBM)] * 5,
        out_specs=[VMEM] * 7,
        out_shape=[block, block, *same, jax.ShapeDtypeStruct((copies, LANES), F32)],
        scratch_shapes=[pltpu.SMEM((copies,), F32), pltpu.SemaphoreType.DMA((5,))],
        compiler_params=SMALL,
        name="pack",
    )(*(pltpu.with_memory_space_constraint(x, pltpu.HBM) for x in (coords_pred, coords_true, kind, partners, noise_level)))
    forward = [(i, i + 1) for i in range(size - 1)]
    low = lax.ppermute(last, "res", forward)
    high = lax.ppermute(first, "res", [(b, a) for a, b in forward])

    shared_shapes = Engine.shared_shapes(tiles, copies)
    count = len(shared_shapes)
    x_shape = pltpu.VMEM((6, 16, LANES), F32)
    *shared, items, moments = pl.pallas_call(
        functools.partial(self_kernel, copies=copies, tiles=tiles),
        in_specs=[SMEM, SMEM] + [VMEM] * 3,
        out_specs=[VMEM] * (count + 2),
        out_shape=[*shared_shapes, jax.ShapeDtypeStruct((1, LANES), jnp.int32), jax.ShapeDtypeStruct((3, 8, LANES), F32)],
        scratch_shapes=[x_shape, pltpu.VMEM((2, 6, 16, LANES), F32), pltpu.VMEM((1, LANES, LANES), BF16), *Engine.work_shapes(copies, 2)],
        compiler_params=PARAMS,
        cost_estimate=pl.CostEstimate(flops=10**8, bytes_accessed=10**6, transcendentals=10**7),
        name="self_tiles",
    )(base, partners, coords_pred, coords_true, kind)
    stats, *shared = pl.pallas_call(
        functools.partial(cross_kernel, copies=copies, tiles=tiles),
        in_specs=[SMEM] + [VMEM] * (3 + count),
        out_specs=[VMEM] * (1 + count),
        out_shape=[stats_shape, *shared_shapes],
        input_output_aliases={4 + i: 1 + i for i in range(count)},
        scratch_shapes=[x_shape, *Engine.work_shapes(copies, 1)],
        compiler_params=PARAMS,
        name="cross_tiles",
    )(items, moments, low, high, *shared)

    step = 1
    while True:
        other = swap(stats, "res", step)
        step *= 2
        if step == size:
            break
        total, error = two_sum(stats[0], other[0])
        stats = jnp.stack([total, (stats[1] + other[1]) + error])

    copy_loss, total, maps, centre = pl.pallas_call(
        functools.partial(solve_kernel, copies=copies, atoms=local * size),
        in_specs=[VMEM] * 3,
        out_specs=[SMEM] + [VMEM] * 3,
        out_shape=[
            jax.ShapeDtypeStruct((copies,), F32),
            jax.ShapeDtypeStruct((8, LANES), F32),
            jax.ShapeDtypeStruct((14, copies, LANES), F32),
            jax.ShapeDtypeStruct((8, LANES), F32),
        ],
        scratch_shapes=[pltpu.VMEM((2, LANES, LANES), F32)],
        compiler_params=SMALL,
        name="solve",
    )(stats, other, noise)
    step = 1
    while step < lax.axis_size("samp"):
        total = total + swap(total, "samp", step)
        step *= 2
    mean_loss = total[0, 0] / (copies * lax.axis_size("samp"))
    grad = pl.pallas_call(
        functools.partial(gradient_kernel, copies=copies, tiles=tiles),
        in_specs=[VMEM] * 6,
        out_specs=VMEM,
        out_shape=jax.ShapeDtypeStruct((3, copies, local), F32),
        cost_estimate=pl.CostEstimate(flops=10**6, bytes_accessed=10**6, transcendentals=0),
        compiler_params=SMALL,
        name="gradient",
    )(maps, centre, coords_pred, coords_true, kind, shared[Engine.shared.index("acc")])
    return copy_loss, mean_loss, jnp.transpose(grad, (1, 0, 2))


def solution(mesh):
    in_specs = (P("samp", None, "res"), P(None, "res"), P("res"), P("res", None), P("samp"))
    out_specs = (P("samp"), P(), P("samp", None, "res"))
    return jax.shard_map(shards, mesh=mesh, in_specs=in_specs, out_specs=out_specs, check_vma=False)
```

profile of v0, /device:TPU:0, one launch (start us, length us, event | category | flops | bytes accessed | tf_op | source)
XLA Modules:
  0.0 53.1 jit_solution(5887830312161488892)
XLA Ops:
  0.6 1.0 %pack.1 = (f32[16,256]{1,0:T(8,128)S(1)}, f32[16,256]{1,0:T(8,128)S(1)}, f32[3,4,3072]{2,1,0:T(4,128)S(1)}, f32[3,3072]{1,0:T(4,128)S(1)}, s32[1,3072]{1,0:T(1,1...) custom-call(f32[3,4,3072]{2,1,0:T(4,128)} %bitcast.6, f32[3,3072]{1,0:T(4,128)} %true_hbm.1, s32[1,3072]{1,0:T(1,128)} %bitcast.8, ...), custom_call_target="tpu_custom_call" | custom-call | tf_op jit(solution)/shard_map/pack/pallas_call | solution.py:627
  1.6 4.8 %collective-permute-start = (f32[16,256]{1,0:T(8,128)S(1)}, f32[16,256]{1,0:T(8,128)S(1)}, u32[]{:S(2)}, u32[]{:S(2)}) collective-permute-start(f32[16,256]{1,0:T(8,128)S(1)} %get-tuple-element.32), channel_id=1, source_target_pairs={{0,4},{4,8},{8,12},{12,16},{16,20},{20,24},{24,28},{1,5},{5,9},{9,... | collective-permute-start | bytes 49160 | tf_op jit(solution)/shard_map/ppermute | solution.py:637
  6.5 1.3 %collective-permute-start.1 = (f32[16,256]{1,0:T(8,128)S(1)}, f32[16,256]{1,0:T(8,128)S(1)}, u32[]{:S(2)}, u32[]{:S(2)}) collective-permute-start(f32[16,256]{1,0:T(8,128)S(1)} %get-tuple-element.33), channel_id=1, source_target_pairs={{4,0},{8,4},{12,8},{16,12},{20,16},{24,20},{28,24},{5,1},{9,5},{13... | collective-permute-start | bytes 49160 | tf_op jit(solution)/shard_map/ppermute | solution.py:638
  7.8 9.7 %self_tiles.1 = (f32[29,5,8,128]{3,2,1,0:T(8,128)S(1)}, f32[29,1,128]{2,1,0:T(1,128)S(1)}, f32[29,5,8,128]{3,2,1,0:T(8,128)S(1)}, bf16[29,3,128,128]{3,2,1,0:T(8...) custom-call(s32[1]{0:T(128)} %bitcast.base_ref, ...), custom_call_target="tpu_custom_call" | custom-call | flops 100000000 | bytes 1000000 | tf_op jit(solution)/shard_map/self_tiles/pallas_call | solution.py:643
  17.5 0.0 collective-permute-done.low_ref
  17.5 0.0 collective-permute-done.1.high_ref
  17.5 11.8 %cross_tiles.1 = (f32[2,8,128]{2,1,0:T(8,128)S(1)}, f32[29,5,8,128]{3,2,1,0:T(8,128)S(1)}, f32[29,1,128]{2,1,0:T(1,128)S(1)}, f32[29,5,8,128]{3,2,1,0:T(8,128)S(...) custom-call(s32[1,128]{1,0:T(1,128)S(1)} %get-tuple-element.30.items, ...), custom_call_target="tpu_custom_call", output_to_operand_aliasing={{1}: (4, {}), {2}: (5, {}), {3}: (6, {}), {4}: (7, {}), {5}... | custom-call | tf_op jit(solution)/shard_map/cross_tiles/pallas_call | solution.py:653
  29.3 2.3 %collective-permute-start.2 = (f32[2,8,128]{2,1,0:T(8,128)S(1)}, f32[2,8,128]{2,1,0:T(8,128)S(1)}, u32[]{:S(2)}, u32[]{:S(2)}) collective-permute-start(f32[2,8,128]{2,1,0:T(8,128)S(1)} %get-tuple-element.42), channel_id=1, source_target_pairs={{0,4},{4,0},{8,12},{12,8},{16,20},{20,16},{24,28},{28,24},{1,5},{5... | collective-permute-start | bytes 24584 | tf_op jit(solution)/shard_map/ppermute | solution.py:611
  31.6 1.6 %collective-permute-done.2 = f32[2,8,128]{2,1,0:T(8,128)S(1)} collective-permute-done((f32[2,8,128]{2,1,0:T(8,128)S(1)}, f32[2,8,128]{2,1,0:T(8,128)S(1)}, u32[]{:S(2)}, u32[]{:S(2)}) %collective-permute-start.2) | collective-permute-done | bytes 8224 | tf_op jit(solution)/shard_map/ppermute | solution.py:611
  33.2 4.3 %collective-permute-start.3 = (f32[2,8,128]{2,1,0:T(8,128)S(1)}, f32[2,8,128]{2,1,0:T(8,128)S(1)}, u32[]{:S(2)}, u32[]{:S(2)}) collective-permute-start(f32[2,8,128]{2,1,0:T(8,128)S(1)} %pad_maximum_fusion), channel_id=1, source_target_pairs={{0,8},{4,12},{8,0},{12,4},{16,24},{20,28},{24,16},{28,20},{1,9},{5... | collective-permute-start | bytes 24584 | tf_op jit(solution)/shard_map/ppermute | solution.py:611
  37.5 1.6 %collective-permute-done.3 = f32[2,8,128]{2,1,0:T(8,128)S(1)} collective-permute-done((f32[2,8,128]{2,1,0:T(8,128)S(1)}, f32[2,8,128]{2,1,0:T(8,128)S(1)}, u32[]{:S(2)}, u32[]{:S(2)}) %collective-permute-start.3) | collective-permute-done | bytes 8224 | tf_op jit(solution)/shard_map/ppermute | solution.py:611
  39.2 3.9 %collective-permute-start.4 = (f32[2,8,128]{2,1,0:T(8,128)S(1)}, f32[2,8,128]{2,1,0:T(8,128)S(1)}, u32[]{:S(2)}, u32[]{:S(2)}) collective-permute-start(f32[2,8,128]{2,1,0:T(8,128)S(1)} %pad_maximum_fusion.1.stat_ref), channel_id=1, source_target_pairs={{0,16},{4,20},{8,24},{12,28},{16,0},{20,4},{24,8},{28,12},{1,17},{... | collective-permute-start | bytes 24584 | tf_op jit(solution)/shard_map/ppermute | solution.py:611
  43.1 1.6 %collective-permute-done.4.other_ref = f32[2,8,128]{2,1,0:T(8,128)S(1)} collective-permute-done((f32[2,8,128]{2,1,0:T(8,128)S(1)}, f32[2,8,128]{2,1,0:T(8,128)S(1)}, u32[]{:S(2)}, u32[]{:S(2)}) %collective-permute-start.4) | collective-permute-done | bytes 8224 | tf_op jit(solution)/shard_map/ppermute | solution.py:611
  44.7 1.2 %solve.1 = (f32[4]{0:T(128)}, f32[8,128]{1,0:T(8,128)S(1)}, f32[14,4,128]{2,1,0:T(4,128)S(1)}, f32[8,128]{1,0:T(8,128)S(1)}) custom-call(f32[2,8,128]{2,1,0:T(8,128)S(1)} %pad_maximum_fusion.1.stat_ref, f32[2,8,128]{2,1,0:T(8,128)S(1)} %collective-permute-done.4.other_ref, f32[4,128]{1,0:T(4,128)S(1)} %get-tuple-element.43.noise_ref), custom_call_target="tpu_custom_call" | custom-call | tf_op jit(solution)/shard_map/solve/pallas_call | solution.py:673
  45.9 0.1 collective-permute-start.5
  46.0 1.2 %collective-permute-done.5 = f32[8,128]{1,0:T(8,128)S(1)} collective-permute-done((f32[8,128]{1,0:T(8,128)S(1)}, f32[8,128]{1,0:T(8,128)S(1)}, u32[]{:S(2)}, u32[]{:S(2)}) %collective-permute-start.5) | collective-permute-done | bytes 4128 | tf_op jit(solution)/shard_map/ppermute | solution.py:611
  47.2 1.5 %collective-permute-start.6 = (f32[8,128]{1,0:T(8,128)S(1)}, f32[8,128]{1,0:T(8,128)S(1)}, u32[]{:S(2)}, u32[]{:S(2)}) collective-permute-start(f32[8,128]{1,0:T(8,128)S(1)} %add.53), channel_id=1, source_target_pairs={{0,2},{1,3},{2,0},{3,1},{4,6},{5,7},{6,4},{7,5},{8,10},{9,11},{10,... | collective-permute-start | bytes 12296 | tf_op jit(solution)/shard_map/ppermute | solution.py:611
  48.7 0.8 %gradient.1 = f32[3,4,3072]{2,1,0:T(4,128)} custom-call(f32[14,4,128]{2,1,0:T(4,128)S(1)} %get-tuple-element.46.m_ref, f32[8,128]{1,0:T(8,128)S(1)} %get-tuple-element.47.k_ref, f32[3,4,3072]{2,1,0:T(4,128)S(1)} %get-tuple-element.27.pred_ref, f32[3,3072]{1,0:T(4,128)S(1)} %get-tuple-element.28.true_ref, s32[1,3072]{1,0:T(1,128)S(1)} %get-tuple-element.29.kind_ref, ...), custom_call_target="tpu_custom_call" | custom-call | flops 1000000 | bytes 1000000 | tf_op jit(solution)/shard_map/gradient/pallas_call | solution.py:692
  49.5 1.3 %collective-permute-done.6 = f32[8,128]{1,0:T(8,128)S(1)} collective-permute-done((f32[8,128]{1,0:T(8,128)S(1)}, f32[8,128]{1,0:T(8,128)S(1)}, u32[]{:S(2)}, u32[]{:S(2)}) %collective-permute-start.6) | collective-permute-done | bytes 4128 | tf_op jit(solution)/shard_map/ppermute | solution.py:611
  50.8 0.5 slice.27
  (6 shorter events, 0.0 us)
Async XLA Ops:
  1.6 15.9 %collective-permute-start = (f32[16,256]{1,0:T(8,128)S(1)}, f32[16,256]{1,0:T(8,128)S(1)}, u32[]{:S(2)}, u32[]{:S(2)}) collective-permute-start(f32[16,256]{1,0:T(8,128)S(1)} %get-tuple-element.32), channel_id=1, source_target_pairs={{0,4},{4,8},{8,12},{12,16},{16,20},{20,24},{24,28},{1,5},{5,9},{9,... | collective-permute-start | bytes 49160 | tf_op jit(solution)/shard_map/ppermute | solution.py:637
  6.5 11.0 %collective-permute-start.1 = (f32[16,256]{1,0:T(8,128)S(1)}, f32[16,256]{1,0:T(8,128)S(1)}, u32[]{:S(2)}, u32[]{:S(2)}) collective-permute-start(f32[16,256]{1,0:T(8,128)S(1)} %get-tuple-element.33), channel_id=1, source_target_pairs={{4,0},{8,4},{12,8},{16,12},{20,16},{24,20},{28,24},{5,1},{9,5},{13... | collective-permute-start | bytes 49160 | tf_op jit(solution)/shard_map/ppermute | solution.py:638
  29.3 3.9 %collective-permute-start.2 = (f32[2,8,128]{2,1,0:T(8,128)S(1)}, f32[2,8,128]{2,1,0:T(8,128)S(1)}, u32[]{:S(2)}, u32[]{:S(2)}) collective-permute-start(f32[2,8,128]{2,1,0:T(8,128)S(1)} %get-tuple-element.42), channel_id=1, source_target_pairs={{0,4},{4,0},{8,12},{12,8},{16,20},{20,16},{24,28},{28,24},{1,5},{5... | collective-permute-start | bytes 24584 | tf_op jit(solution)/shard_map/ppermute | solution.py:611
  33.2 5.9 %collective-permute-start.3 = (f32[2,8,128]{2,1,0:T(8,128)S(1)}, f32[2,8,128]{2,1,0:T(8,128)S(1)}, u32[]{:S(2)}, u32[]{:S(2)}) collective-permute-start(f32[2,8,128]{2,1,0:T(8,128)S(1)} %pad_maximum_fusion), channel_id=1, source_target_pairs={{0,8},{4,12},{8,0},{12,4},{16,24},{20,28},{24,16},{28,20},{1,9},{5... | collective-permute-start | bytes 24584 | tf_op jit(solution)/shard_map/ppermute | solution.py:611
  39.2 5.6 %collective-permute-start.4 = (f32[2,8,128]{2,1,0:T(8,128)S(1)}, f32[2,8,128]{2,1,0:T(8,128)S(1)}, u32[]{:S(2)}, u32[]{:S(2)}) collective-permute-start(f32[2,8,128]{2,1,0:T(8,128)S(1)} %pad_maximum_fusion.1.stat_ref), channel_id=1, source_target_pairs={{0,16},{4,20},{8,24},{12,28},{16,0},{20,4},{24,8},{28,12},{1,17},{... | collective-permute-start | bytes 24584 | tf_op jit(solution)/shard_map/ppermute | solution.py:611
  45.9 1.2 %collective-permute-start.5 = (f32[8,128]{1,0:T(8,128)S(1)}, f32[8,128]{1,0:T(8,128)S(1)}, u32[]{:S(2)}, u32[]{:S(2)}) collective-permute-start(f32[8,128]{1,0:T(8,128)S(1)} %get-tuple-element.45), channel_id=1, source_target_pairs={{0,1},{1,0},{2,3},{3,2},{4,5},{5,4},{6,7},{7,6},{8,9},{9,8},{10,11... | collective-permute-start | bytes 12296 | tf_op jit(solution)/shard_map/ppermute | solution.py:611
  47.2 3.6 %collective-permute-start.6 = (f32[8,128]{1,0:T(8,128)S(1)}, f32[8,128]{1,0:T(8,128)S(1)}, u32[]{:S(2)}, u32[]{:S(2)}) collective-permute-start(f32[8,128]{1,0:T(8,128)S(1)} %add.53), channel_id=1, source_target_pairs={{0,2},{1,3},{2,0},{3,1},{4,6},{5,7},{6,4},{7,5},{8,10},{9,11},{10,... | collective-permute-start | bytes 12296 | tf_op jit(solution)/shard_map/ppermute | solution.py:611
where the time goes:
time: 53.4 us; the launch traced here: 53.1 us
  Pallas kernels  24.5 us (46%)
  starting transfers between devices  18.2 us (34%)
  waiting for transfers between devices  7.32 us (14%)
  between operations  2.48 us (5%)
    ppermute x5, starting transfers between devices, swap(): lax.ppermute(x, axis, [(i, i ^ step) for i in range(lax.axis_size(axis))])  12.1 us
    pallas_call x1, Pallas kernels, shards(): pl.pallas_call(functools.partial(cross_kernel, copies=copies, tiles=tiles...  11.8 us
    pallas_call x1, Pallas kernels, shards(): pl.pallas_call(functools.partial(self_kernel, copies=copies, tiles=tiles)...  9.7 us
    ppermute x5, waiting for transfers between devices, swap(): lax.ppermute(x, axis, [(i, i ^ step) for i in range(lax.axis_size(axis))])  7.31 us
    ppermute x1, starting transfers between devices, shards(): low = lax.ppermute(last, 'res', forward)  4.84 us
    ppermute x1, starting transfers between devices, shards(): high = lax.ppermute(first, 'res', [(b, a) for a, b in forward])  1.29 us
    pallas_call x1, Pallas kernels, shards(): pl.pallas_call(functools.partial(solve_kernel, copies=copies, atoms=local...  1.17 us
  transfers between devices with their start and end apart: 7, of which 5 were waited for; matrix products, arithmetic and copies ran while one was open for 0% of the time, Pallas kernels for 20%

commit v1 on v0

--- a/solution.py
+++ b/solution.py
@@ -557,7 +557,7 @@
         for d in range(3):
             m_ref[3 * c + d] = x[c][d]
         m_ref[9 + c] = pred_mean[c][0]
-        k_ref[c:c + 1, :] = true_mean[c][0][0:1]
+    k_ref[...] = sum(true_mean[c][0][0:1] * Engine.unit(c) for c in range(3))
     m_ref[12] = grad_scale * 2.0 * loss_weight / (3.0 * weight_sum)
     m_ref[13] = grad_scale / count
 
@@ -590,10 +590,8 @@
         move.wait()
     for ref, start in ((first_ref, 0), (last_ref, tiles * LANES - span)):
         sl = slice(start, start + span)
-        for c in range(3):
-            ref[c * copies:(c + 1) * copies, :] = pred_ref[c, :, sl] * 0.5
-        ref[3 * copies:3 * copies + 3, :] = true_ref[:, sl] * 0.5
-        ref[3 * copies + 3:3 * copies + 4, :] = jnp.where(kind_ref[:, sl] == 1, 15.0, 7.5)
+        cut = jnp.where(kind_ref[:, sl] == 1, 15.0, 7.5)
+        ref[...] = jnp.concatenate([pred_ref[c, :, sl] * 0.5 for c in range(3)] + [true_ref[:, sl] * 0.5, cut], axis=0)
     row = lax.broadcasted_iota(jnp.int32, (copies, LANES), 0)
     noise = jnp.zeros((copies, LANES), F32)
     for s in range(copies):
@@ -639,7 +637,7 @@
 
     shared_shapes = Engine.shared_shapes(tiles, copies)
     count = len(shared_shapes)
-    x_shape = pltpu.VMEM((6, 16, LANES), F32)
+    x_shape = pltpu.VMEM((8, 16, LANES), F32)
     *shared, items, moments = pl.pallas_call(
         functools.partial(self_kernel, copies=copies, tiles=tiles),
         in_specs=[SMEM, SMEM] + [VMEM] * 3,

time: 53.4 us -> 53.6 us (level); the launches traced: 53.1 us -> 53.9 us
  starting transfers between devices: 18.2 us -> 20.8 us
  Pallas kernels: 24.5 us -> 22.8 us
    ppermute x5, starting transfers between devices: 12.1 us -> 14.7 us  [swap(): lax.ppermute(x, axis, [(i, i ^ step) for i in range(lax.axis_size(axis))])]
    pallas_call x1, Pallas kernels: 11.8 us -> 10.1 us  [shards(): pl.pallas_call(functools.partial(cross_kernel, copies=copies, tiles=tiles...]
where the time goes in v1:
time: 53.6 us; the launch traced here: 53.9 us
  Pallas kernels  22.8 us (43%)
  starting transfers between devices  20.8 us (39%)
  waiting for transfers between devices  7.32 us (14%)
  between operations  2.48 us (5%)
    ppermute x5, starting transfers between devices, swap(): lax.ppermute(x, axis, [(i, i ^ step) for i in range(lax.axis_size(axis))])  14.7 us
    pallas_call x1, Pallas kernels, shards(): pl.pallas_call(functools.partial(cross_kernel, copies=copies, tiles=tiles...  10.1 us
    pallas_call x1, Pallas kernels, shards(): pl.pallas_call(functools.partial(self_kernel, copies=copies, tiles=tiles)...  9.7 us
    ppermute x5, waiting for transfers between devices, swap(): lax.ppermute(x, axis, [(i, i ^ step) for i in range(lax.axis_size(axis))])  7.31 us
    ppermute x1, starting transfers between devices, shards(): low = lax.ppermute(last, 'res', forward)  4.84 us
    ppermute x1, starting transfers between devices, shards(): high = lax.ppermute(first, 'res', [(b, a) for a, b in forward])  1.29 us
    pallas_call x1, Pallas kernels, shards(): pl.pallas_call(functools.partial(solve_kernel, copies=copies, atoms=local...  1.17 us
  transfers between devices with their start and end apart: 7, of which 5 were waited for; matrix products, arithmetic and copies ran while one was open for 0% of the time, Pallas kernels for 20%

profile of v1, /device:TPU:0, one launch (start us, length us, event | category | flops | bytes accessed | tf_op | source)
XLA Modules:
  0.0 53.9 jit_solution(10763619109346674333)
XLA Ops:
  0.6 1.0 %pack.1 = (f32[16,256]{1,0:T(8,128)S(1)}, f32[16,256]{1,0:T(8,128)S(1)}, f32[3,4,3072]{2,1,0:T(4,128)S(1)}, f32[3,3072]{1,0:T(4,128)S(1)}, s32[1,3072]{1,0:T(1,1...) custom-call(f32[3,4,3072]{2,1,0:T(4,128)} %bitcast.6, f32[3,3072]{1,0:T(4,128)} %true_hbm.1, s32[1,3072]{1,0:T(1,128)} %bitcast.8, ...), custom_call_target="tpu_custom_call" | custom-call | tf_op jit(solution)/shard_map/pack/pallas_call | solution.py:625
  1.6 4.8 %collective-permute-start = (f32[16,256]{1,0:T(8,128)S(1)}, f32[16,256]{1,0:T(8,128)S(1)}, u32[]{:S(2)}, u32[]{:S(2)}) collective-permute-start(f32[16,256]{1,0:T(8,128)S(1)} %get-tuple-element.32), channel_id=1, source_target_pairs={{0,4},{4,8},{8,12},{12,16},{16,20},{20,24},{24,28},{1,5},{5,9},{9,... | collective-permute-start | bytes 49160 | tf_op jit(solution)/shard_map/ppermute | solution.py:635
  6.5 1.3 %collective-permute-start.1 = (f32[16,256]{1,0:T(8,128)S(1)}, f32[16,256]{1,0:T(8,128)S(1)}, u32[]{:S(2)}, u32[]{:S(2)}) collective-permute-start(f32[16,256]{1,0:T(8,128)S(1)} %get-tuple-element.33), channel_id=1, source_target_pairs={{4,0},{8,4},{12,8},{16,12},{20,16},{24,20},{28,24},{5,1},{9,5},{13... | collective-permute-start | bytes 49160 | tf_op jit(solution)/shard_map/ppermute | solution.py:636
  7.8 9.7 %self_tiles.1 = (f32[29,5,8,128]{3,2,1,0:T(8,128)S(1)}, f32[29,1,128]{2,1,0:T(1,128)S(1)}, f32[29,5,8,128]{3,2,1,0:T(8,128)S(1)}, bf16[29,3,128,128]{3,2,1,0:T(8...) custom-call(s32[1]{0:T(128)} %bitcast.base_ref, ...), custom_call_target="tpu_custom_call" | custom-call | flops 100000000 | bytes 1000000 | tf_op jit(solution)/shard_map/self_tiles/pallas_call | solution.py:641
  17.5 0.0 collective-permute-done.low_ref
  17.5 0.0 collective-permute-done.1.high_ref
  17.5 10.1 %cross_tiles.1 = (f32[2,8,128]{2,1,0:T(8,128)S(1)}, f32[29,5,8,128]{3,2,1,0:T(8,128)S(1)}, f32[29,1,128]{2,1,0:T(1,128)S(1)}, f32[29,5,8,128]{3,2,1,0:T(8,128)S(...) custom-call(s32[1,128]{1,0:T(1,128)S(1)} %get-tuple-element.30.items, ...), custom_call_target="tpu_custom_call", output_to_operand_aliasing={{1}: (4, {}), {2}: (5, {}), {3}: (6, {}), {4}: (7, {}), {5}... | custom-call | tf_op jit(solution)/shard_map/cross_tiles/pallas_call | solution.py:651
  27.6 3.1 %collective-permute-start.2 = (f32[2,8,128]{2,1,0:T(8,128)S(1)}, f32[2,8,128]{2,1,0:T(8,128)S(1)}, u32[]{:S(2)}, u32[]{:S(2)}) collective-permute-start(f32[2,8,128]{2,1,0:T(8,128)S(1)} %get-tuple-element.42), channel_id=1, source_target_pairs={{0,4},{4,0},{8,12},{12,8},{16,20},{20,16},{24,28},{28,24},{1,5},{5... | collective-permute-start | bytes 24584 | tf_op jit(solution)/shard_map/ppermute | solution.py:609
  30.7 1.6 %collective-permute-done.2 = f32[2,8,128]{2,1,0:T(8,128)S(1)} collective-permute-done((f32[2,8,128]{2,1,0:T(8,128)S(1)}, f32[2,8,128]{2,1,0:T(8,128)S(1)}, u32[]{:S(2)}, u32[]{:S(2)}) %collective-permute-start.2) | collective-permute-done | bytes 8224 | tf_op jit(solution)/shard_map/ppermute | solution.py:609
  32.4 3.1 %collective-permute-start.3 = (f32[2,8,128]{2,1,0:T(8,128)S(1)}, f32[2,8,128]{2,1,0:T(8,128)S(1)}, u32[]{:S(2)}, u32[]{:S(2)}) collective-permute-start(f32[2,8,128]{2,1,0:T(8,128)S(1)} %pad_maximum_fusion), channel_id=1, source_target_pairs={{0,8},{4,12},{8,0},{12,4},{16,24},{20,28},{24,16},{28,20},{1,9},{5... | collective-permute-start | bytes 24584 | tf_op jit(solution)/shard_map/ppermute | solution.py:609
  35.4 1.6 %collective-permute-done.3 = f32[2,8,128]{2,1,0:T(8,128)S(1)} collective-permute-done((f32[2,8,128]{2,1,0:T(8,128)S(1)}, f32[2,8,128]{2,1,0:T(8,128)S(1)}, u32[]{:S(2)}, u32[]{:S(2)}) %collective-permute-start.3) | collective-permute-done | bytes 8224 | tf_op jit(solution)/shard_map/ppermute | solution.py:609
  37.1 6.9 %collective-permute-start.4 = (f32[2,8,128]{2,1,0:T(8,128)S(1)}, f32[2,8,128]{2,1,0:T(8,128)S(1)}, u32[]{:S(2)}, u32[]{:S(2)}) collective-permute-start(f32[2,8,128]{2,1,0:T(8,128)S(1)} %pad_maximum_fusion.1.stat_ref), channel_id=1, source_target_pairs={{0,16},{4,20},{8,24},{12,28},{16,0},{20,4},{24,8},{28,12},{1,17},{... | collective-permute-start | bytes 24584 | tf_op jit(solution)/shard_map/ppermute | solution.py:609
  44.0 1.6 %collective-permute-done.4.other_ref = f32[2,8,128]{2,1,0:T(8,128)S(1)} collective-permute-done((f32[2,8,128]{2,1,0:T(8,128)S(1)}, f32[2,8,128]{2,1,0:T(8,128)S(1)}, u32[]{:S(2)}, u32[]{:S(2)}) %collective-permute-start.4) | collective-permute-done | bytes 8224 | tf_op jit(solution)/shard_map/ppermute | solution.py:609
  45.6 1.2 %solve.1 = (f32[4]{0:T(128)}, f32[8,128]{1,0:T(8,128)S(1)}, f32[14,4,128]{2,1,0:T(4,128)S(1)}, f32[8,128]{1,0:T(8,128)S(1)}) custom-call(f32[2,8,128]{2,1,0:T(8,128)S(1)} %pad_maximum_fusion.1.stat_ref, f32[2,8,128]{2,1,0:T(8,128)S(1)} %collective-permute-done.4.other_ref, f32[4,128]{1,0:T(4,128)S(1)} %get-tuple-element.43.noise_ref), custom_call_target="tpu_custom_call" | custom-call | tf_op jit(solution)/shard_map/solve/pallas_call | solution.py:671
  46.8 0.1 collective-permute-start.5
  46.9 1.2 %collective-permute-done.5 = f32[8,128]{1,0:T(8,128)S(1)} collective-permute-done((f32[8,128]{1,0:T(8,128)S(1)}, f32[8,128]{1,0:T(8,128)S(1)}, u32[]{:S(2)}, u32[]{:S(2)}) %collective-permute-start.5) | collective-permute-done | bytes 4128 | tf_op jit(solution)/shard_map/ppermute | solution.py:609
  48.0 1.5 %collective-permute-start.6 = (f32[8,128]{1,0:T(8,128)S(1)}, f32[8,128]{1,0:T(8,128)S(1)}, u32[]{:S(2)}, u32[]{:S(2)}) collective-permute-start(f32[8,128]{1,0:T(8,128)S(1)} %add.53), channel_id=1, source_target_pairs={{0,2},{1,3},{2,0},{3,1},{4,6},{5,7},{6,4},{7,5},{8,10},{9,11},{10,... | collective-permute-start | bytes 12296 | tf_op jit(solution)/shard_map/ppermute | solution.py:609
  49.5 0.8 %gradient.1 = f32[3,4,3072]{2,1,0:T(4,128)} custom-call(f32[14,4,128]{2,1,0:T(4,128)S(1)} %get-tuple-element.46.m_ref, f32[8,128]{1,0:T(8,128)S(1)} %get-tuple-element.47.k_ref, f32[3,4,3072]{2,1,0:T(4,128)S(1)} %get-tuple-element.27.pred_ref, f32[3,3072]{1,0:T(4,128)S(1)} %get-tuple-element.28.true_ref, s32[1,3072]{1,0:T(1,128)S(1)} %get-tuple-element.29.kind_ref, ...), custom_call_target="tpu_custom_call" | custom-call | flops 1000000 | bytes 1000000 | tf_op jit(solution)/shard_map/gradient/pallas_call | solution.py:690
  50.3 1.3 %collective-permute-done.6 = f32[8,128]{1,0:T(8,128)S(1)} collective-permute-done((f32[8,128]{1,0:T(8,128)S(1)}, f32[8,128]{1,0:T(8,128)S(1)}, u32[]{:S(2)}, u32[]{:S(2)}) %collective-permute-start.6) | collective-permute-done | bytes 4128 | tf_op jit(solution)/shard_map/ppermute | solution.py:609
  51.6 0.5 slice.27
  (6 shorter events, 0.0 us)
Async XLA Ops:
  1.6 15.9 %collective-permute-start = (f32[16,256]{1,0:T(8,128)S(1)}, f32[16,256]{1,0:T(8,128)S(1)}, u32[]{:S(2)}, u32[]{:S(2)}) collective-permute-start(f32[16,256]{1,0:T(8,128)S(1)} %get-tuple-element.32), channel_id=1, source_target_pairs={{0,4},{4,8},{8,12},{12,16},{16,20},{20,24},{24,28},{1,5},{5,9},{9,... | collective-permute-start | bytes 49160 | tf_op jit(solution)/shard_map/ppermute | solution.py:635
  6.5 11.0 %collective-permute-start.1 = (f32[16,256]{1,0:T(8,128)S(1)}, f32[16,256]{1,0:T(8,128)S(1)}, u32[]{:S(2)}, u32[]{:S(2)}) collective-permute-start(f32[16,256]{1,0:T(8,128)S(1)} %get-tuple-element.33), channel_id=1, source_target_pairs={{4,0},{8,4},{12,8},{16,12},{20,16},{24,20},{28,24},{5,1},{9,5},{13... | collective-permute-start | bytes 49160 | tf_op jit(solution)/shard_map/ppermute | solution.py:636
  27.6 4.8 %collective-permute-start.2 = (f32[2,8,128]{2,1,0:T(8,128)S(1)}, f32[2,8,128]{2,1,0:T(8,128)S(1)}, u32[]{:S(2)}, u32[]{:S(2)}) collective-permute-start(f32[2,8,128]{2,1,0:T(8,128)S(1)} %get-tuple-element.42), channel_id=1, source_target_pairs={{0,4},{4,0},{8,12},{12,8},{16,20},{20,16},{24,28},{28,24},{1,5},{5... | collective-permute-start | bytes 24584 | tf_op jit(solution)/shard_map/ppermute | solution.py:609
  32.4 4.7 %collective-permute-start.3 = (f32[2,8,128]{2,1,0:T(8,128)S(1)}, f32[2,8,128]{2,1,0:T(8,128)S(1)}, u32[]{:S(2)}, u32[]{:S(2)}) collective-permute-start(f32[2,8,128]{2,1,0:T(8,128)S(1)} %pad_maximum_fusion), channel_id=1, source_target_pairs={{0,8},{4,12},{8,0},{12,4},{16,24},{20,28},{24,16},{28,20},{1,9},{5... | collective-permute-start | bytes 24584 | tf_op jit(solution)/shard_map/ppermute | solution.py:609
  37.1 8.5 %collective-permute-start.4 = (f32[2,8,128]{2,1,0:T(8,128)S(1)}, f32[2,8,128]{2,1,0:T(8,128)S(1)}, u32[]{:S(2)}, u32[]{:S(2)}) collective-permute-start(f32[2,8,128]{2,1,0:T(8,128)S(1)} %pad_maximum_fusion.1.stat_ref), channel_id=1, source_target_pairs={{0,16},{4,20},{8,24},{12,28},{16,0},{20,4},{24,8},{28,12},{1,17},{... | collective-permute-start | bytes 24584 | tf_op jit(solution)/shard_map/ppermute | solution.py:609
  46.8 1.2 %collective-permute-start.5 = (f32[8,128]{1,0:T(8,128)S(1)}, f32[8,128]{1,0:T(8,128)S(1)}, u32[]{:S(2)}, u32[]{:S(2)}) collective-permute-start(f32[8,128]{1,0:T(8,128)S(1)} %get-tuple-element.45), channel_id=1, source_target_pairs={{0,1},{1,0},{2,3},{3,2},{4,5},{5,4},{6,7},{7,6},{8,9},{9,8},{10,11... | collective-permute-start | bytes 12296 | tf_op jit(solution)/shard_map/ppermute | solution.py:609
  48.0 3.6 %collective-permute-start.6 = (f32[8,128]{1,0:T(8,128)S(1)}, f32[8,128]{1,0:T(8,128)S(1)}, u32[]{:S(2)}, u32[]{:S(2)}) collective-permute-start(f32[8,128]{1,0:T(8,128)S(1)} %add.53), channel_id=1, source_target_pairs={{0,2},{1,3},{2,0},{3,1},{4,6},{5,7},{6,4},{7,5},{8,10},{9,11},{10,... | collective-permute-start | bytes 12296 | tf_op jit(solution)/shard_map/ppermute | solution.py:609

commit v2 on v1

--- a/solution.py
+++ b/solution.py
@@ -157,7 +157,7 @@
             self.centre[t, s] = centre
             y = v - centre
             norm = jnp.sum(y * y, axis=0, keepdims=True)
-            x = y + (self.unit(4) + EPS * self.unit(5)) + norm * self.unit(3)
+            x = (self.unit(4) + EPS * self.unit(5)) - 2.0 * y + norm * self.unit(3)
             if s == self.copies:
                 x = x + self.unit(7) * self.cut[t]
             a, b, c = split3(x)
@@ -175,7 +175,7 @@
     def build(self, slot, k, g, j, s):
         y = self.v[j, s] - self.centre[g, s]
         norm = jnp.sum(y * y, axis=0, keepdims=True)
-        a, b, c = split3((self.unit(3) + self.unit(5)) - 2.0 * y + norm * self.unit(4))
+        a, b, c = split3(y + (self.unit(3) + self.unit(5)) + norm * self.unit(4))
         q, m = 64 * (s % 2), LANES * (s % 2)
         self.right[slot][k, s // 2, q:q + 64, m:m + LANES] = jnp.concatenate([a, b, a, c, b, a, c, b], axis=0).astype(BF16)
 
@@ -328,11 +328,13 @@
         def at(p):
             return tuple(jnp.where(p < 0, dummy, z) for z in item(jnp.clip(p, 0, n - 1)))
 
-        @pl.loop(0, n // 2)
+        run = 4 if isinstance(n, int) and n % 4 == 0 else 2
+
+        @pl.loop(0, n // run)
         def _(i):
-            p = 2 * i
-            for slot in range(2):
-                self.half(kind, [at(p + slot - 1), at(p + slot), at(p + slot + 1), at(p + slot + 3)], slot)
+            for k in range(run):
+                p = run * i + k
+                self.half(kind, [at(p - 1), at(p), at(p + 1), at(p + 3)], k % 2)
 
     def end_list(self, kind, item, n, dummy):
         def last(i, slot):
@@ -390,7 +392,7 @@
             bits = bits | lax.shift_left(jnp.int32(1), (part_ref[k, t] - base) - (t - BAND))
         return lambda offset: lax.shift_right_logical(bits, BAND + offset) & 1
 
-    unroll = next(u for u in (6, 4, 3, 2, 1) if tiles % u == 0)
+    unroll = next(u for u in (12, 6, 4, 3, 2, 1) if tiles % u == 0)
 
     @pl.loop(0, tiles // unroll)
     def _(m):
@@ -637,7 +639,7 @@
 
     shared_shapes = Engine.shared_shapes(tiles, copies)
     count = len(shared_shapes)
-    x_shape = pltpu.VMEM((8, 16, LANES), F32)
+    x_shape = pltpu.VMEM((14, 16, LANES), F32)
     *shared, items, moments = pl.pallas_call(
         functools.partial(self_kernel, copies=copies, tiles=tiles),
         in_specs=[SMEM, SMEM] + [VMEM] * 3,

time: 53.6 us -> 53.6 us (level); the launches traced: 53.9 us -> 53 us
  starting transfers between devices: 20.8 us -> 17.4 us
  Pallas kernels: 22.8 us -> 24.9 us
    ppermute x5, starting transfers between devices: 14.7 us -> 11.3 us  [swap(): lax.ppermute(x, axis, [(i, i ^ step) for i in range(lax.axis_size(axis))])]
    pallas_call x1, Pallas kernels: 10.1 us -> 12.4 us  [shards(): pl.pallas_call(functools.partial(cross_kernel, copies=copies, tiles=tiles...]
  transfers between devices with their start and end apart: 7 -> 7, of which waited for: 5 -> 5; matrix products, arithmetic and copies ran while one was open for 0% -> 0% of each run, Pallas kernels for 20% -> 19%
where the time goes in v2:
time: 53.6 us; the launch traced here: 53 us
  Pallas kernels  24.9 us (46%)
  starting transfers between devices  17.4 us (32%)
  waiting for transfers between devices  7.67 us (14%)
  between operations  2.48 us (5%)
    pallas_call x1, Pallas kernels, shards(): pl.pallas_call(functools.partial(cross_kernel, copies=copies, tiles=tiles...  12.4 us
    ppermute x5, starting transfers between devices, swap(): lax.ppermute(x, axis, [(i, i ^ step) for i in range(lax.axis_size(axis))])  11.3 us
    pallas_call x1, Pallas kernels, shards(): pl.pallas_call(functools.partial(self_kernel, copies=copies, tiles=tiles)...  9.5 us
    ppermute x5, waiting for transfers between devices, swap(): lax.ppermute(x, axis, [(i, i ^ step) for i in range(lax.axis_size(axis))])  7.66 us
    ppermute x1, starting transfers between devices, shards(): low = lax.ppermute(last, 'res', forward)  4.84 us
    ppermute x1, starting transfers between devices, shards(): high = lax.ppermute(first, 'res', [(b, a) for a, b in forward])  1.29 us
    pallas_call x1, Pallas kernels, shards(): pl.pallas_call(functools.partial(solve_kernel, copies=copies, atoms=local...  1.17 us
  transfers between devices with their start and end apart: 7, of which 5 were waited for; matrix products, arithmetic and copies ran while one was open for 0% of the time, Pallas kernels for 19%

profile of v2, /device:TPU:0, one launch (start us, length us, event | category | flops | bytes accessed | tf_op | source)
XLA Modules:
  0.0 53.0 jit_solution(9375639929611287295)
XLA Ops:
  0.6 1.0 %pack.1 = (f32[16,256]{1,0:T(8,128)S(1)}, f32[16,256]{1,0:T(8,128)S(1)}, f32[3,4,3072]{2,1,0:T(4,128)S(1)}, f32[3,3072]{1,0:T(4,128)S(1)}, s32[1,3072]{1,0:T(1,1...) custom-call(f32[3,4,3072]{2,1,0:T(4,128)} %bitcast.6, f32[3,3072]{1,0:T(4,128)} %true_hbm.1, s32[1,3072]{1,0:T(1,128)} %bitcast.8, ...), custom_call_target="tpu_custom_call" | custom-call | tf_op jit(solution)/shard_map/pack/pallas_call | solution.py:627
  1.6 4.8 %collective-permute-start = (f32[16,256]{1,0:T(8,128)S(1)}, f32[16,256]{1,0:T(8,128)S(1)}, u32[]{:S(2)}, u32[]{:S(2)}) collective-permute-start(f32[16,256]{1,0:T(8,128)S(1)} %get-tuple-element.32), channel_id=1, source_target_pairs={{0,4},{4,8},{8,12},{12,16},{16,20},{20,24},{24,28},{1,5},{5,9},{9,... | collective-permute-start | bytes 49160 | tf_op jit(solution)/shard_map/ppermute | solution.py:637
  6.5 1.3 %collective-permute-start.1 = (f32[16,256]{1,0:T(8,128)S(1)}, f32[16,256]{1,0:T(8,128)S(1)}, u32[]{:S(2)}, u32[]{:S(2)}) collective-permute-start(f32[16,256]{1,0:T(8,128)S(1)} %get-tuple-element.33), channel_id=1, source_target_pairs={{4,0},{8,4},{12,8},{16,12},{20,16},{24,20},{28,24},{5,1},{9,5},{13... | collective-permute-start | bytes 49160 | tf_op jit(solution)/shard_map/ppermute | solution.py:638
  7.8 9.5 %self_tiles.1 = (f32[29,5,8,128]{3,2,1,0:T(8,128)S(1)}, f32[29,1,128]{2,1,0:T(1,128)S(1)}, f32[29,5,8,128]{3,2,1,0:T(8,128)S(1)}, bf16[29,3,128,128]{3,2,1,0:T(8...) custom-call(s32[1]{0:T(128)} %bitcast.base_ref, ...), custom_call_target="tpu_custom_call" | custom-call | flops 100000000 | bytes 1000000 | tf_op jit(solution)/shard_map/self_tiles/pallas_call | solution.py:643
  17.3 0.0 collective-permute-done.low_ref
  17.3 0.0 collective-permute-done.1.high_ref
  17.3 12.4 %cross_tiles.1 = (f32[2,8,128]{2,1,0:T(8,128)S(1)}, f32[29,5,8,128]{3,2,1,0:T(8,128)S(1)}, f32[29,1,128]{2,1,0:T(1,128)S(1)}, f32[29,5,8,128]{3,2,1,0:T(8,128)S(...) custom-call(s32[1,128]{1,0:T(1,128)S(1)} %get-tuple-element.30.items, ...), custom_call_target="tpu_custom_call", output_to_operand_aliasing={{1}: (4, {}), {2}: (5, {}), {3}: (6, {}), {4}: (7, {}), {5}... | custom-call | tf_op jit(solution)/shard_map/cross_tiles/pallas_call | solution.py:653
  29.7 2.7 %collective-permute-start.2 = (f32[2,8,128]{2,1,0:T(8,128)S(1)}, f32[2,8,128]{2,1,0:T(8,128)S(1)}, u32[]{:S(2)}, u32[]{:S(2)}) collective-permute-start(f32[2,8,128]{2,1,0:T(8,128)S(1)} %get-tuple-element.42), channel_id=1, source_target_pairs={{0,4},{4,0},{8,12},{12,8},{16,20},{20,16},{24,28},{28,24},{1,5},{5... | collective-permute-start | bytes 24584 | tf_op jit(solution)/shard_map/ppermute | solution.py:611
  32.4 1.6 %collective-permute-done.2 = f32[2,8,128]{2,1,0:T(8,128)S(1)} collective-permute-done((f32[2,8,128]{2,1,0:T(8,128)S(1)}, f32[2,8,128]{2,1,0:T(8,128)S(1)}, u32[]{:S(2)}, u32[]{:S(2)}) %collective-permute-start.2) | collective-permute-done | bytes 8224 | tf_op jit(solution)/shard_map/ppermute | solution.py:611
  34.0 1.7 %collective-permute-start.3 = (f32[2,8,128]{2,1,0:T(8,128)S(1)}, f32[2,8,128]{2,1,0:T(8,128)S(1)}, u32[]{:S(2)}, u32[]{:S(2)}) collective-permute-start(f32[2,8,128]{2,1,0:T(8,128)S(1)} %pad_maximum_fusion), channel_id=1, source_target_pairs={{0,8},{4,12},{8,0},{12,4},{16,24},{20,28},{24,16},{28,20},{1,9},{5... | collective-permute-start | bytes 24584 | tf_op jit(solution)/shard_map/ppermute | solution.py:611
  35.8 2.0 %collective-permute-done.3 = f32[2,8,128]{2,1,0:T(8,128)S(1)} collective-permute-done((f32[2,8,128]{2,1,0:T(8,128)S(1)}, f32[2,8,128]{2,1,0:T(8,128)S(1)}, u32[]{:S(2)}, u32[]{:S(2)}) %collective-permute-start.3) | collective-permute-done | bytes 8224 | tf_op jit(solution)/shard_map/ppermute | solution.py:611
  37.8 5.3 %collective-permute-start.4 = (f32[2,8,128]{2,1,0:T(8,128)S(1)}, f32[2,8,128]{2,1,0:T(8,128)S(1)}, u32[]{:S(2)}, u32[]{:S(2)}) collective-permute-start(f32[2,8,128]{2,1,0:T(8,128)S(1)} %pad_maximum_fusion.1.stat_ref), channel_id=1, source_target_pairs={{0,16},{4,20},{8,24},{12,28},{16,0},{20,4},{24,8},{28,12},{1,17},{... | collective-permute-start | bytes 24584 | tf_op jit(solution)/shard_map/ppermute | solution.py:611
  43.1 1.6 %collective-permute-done.4.other_ref = f32[2,8,128]{2,1,0:T(8,128)S(1)} collective-permute-done((f32[2,8,128]{2,1,0:T(8,128)S(1)}, f32[2,8,128]{2,1,0:T(8,128)S(1)}, u32[]{:S(2)}, u32[]{:S(2)}) %collective-permute-start.4) | collective-permute-done | bytes 8224 | tf_op jit(solution)/shard_map/ppermute | solution.py:611
  44.7 1.2 %solve.1 = (f32[4]{0:T(128)}, f32[8,128]{1,0:T(8,128)S(1)}, f32[14,4,128]{2,1,0:T(4,128)S(1)}, f32[8,128]{1,0:T(8,128)S(1)}) custom-call(f32[2,8,128]{2,1,0:T(8,128)S(1)} %pad_maximum_fusion.1.stat_ref, f32[2,8,128]{2,1,0:T(8,128)S(1)} %collective-permute-done.4.other_ref, f32[4,128]{1,0:T(4,128)S(1)} %get-tuple-element.43.noise_ref), custom_call_target="tpu_custom_call" | custom-call | tf_op jit(solution)/shard_map/solve/pallas_call | solution.py:673
  45.9 0.1 collective-permute-start.5
  46.0 1.2 %collective-permute-done.5 = f32[8,128]{1,0:T(8,128)S(1)} collective-permute-done((f32[8,128]{1,0:T(8,128)S(1)}, f32[8,128]{1,0:T(8,128)S(1)}, u32[]{:S(2)}, u32[]{:S(2)}) %collective-permute-start.5) | collective-permute-done | bytes 4128 | tf_op jit(solution)/shard_map/ppermute | solution.py:611
  47.1 1.5 %collective-permute-start.6 = (f32[8,128]{1,0:T(8,128)S(1)}, f32[8,128]{1,0:T(8,128)S(1)}, u32[]{:S(2)}, u32[]{:S(2)}) collective-permute-start(f32[8,128]{1,0:T(8,128)S(1)} %add.53), channel_id=1, source_target_pairs={{0,2},{1,3},{2,0},{3,1},{4,6},{5,7},{6,4},{7,5},{8,10},{9,11},{10,... | collective-permute-start | bytes 12296 | tf_op jit(solution)/shard_map/ppermute | solution.py:611
  48.6 0.8 %gradient.1 = f32[3,4,3072]{2,1,0:T(4,128)} custom-call(f32[14,4,128]{2,1,0:T(4,128)S(1)} %get-tuple-element.46.m_ref, f32[8,128]{1,0:T(8,128)S(1)} %get-tuple-element.47.k_ref, f32[3,4,3072]{2,1,0:T(4,128)S(1)} %get-tuple-element.27.pred_ref, f32[3,3072]{1,0:T(4,128)S(1)} %get-tuple-element.28.true_ref, s32[1,3072]{1,0:T(1,128)S(1)} %get-tuple-element.29.kind_ref, ...), custom_call_target="tpu_custom_call" | custom-call | flops 1000000 | bytes 1000000 | tf_op jit(solution)/shard_map/gradient/pallas_call | solution.py:692
  49.5 1.3 %collective-permute-done.6 = f32[8,128]{1,0:T(8,128)S(1)} collective-permute-done((f32[8,128]{1,0:T(8,128)S(1)}, f32[8,128]{1,0:T(8,128)S(1)}, u32[]{:S(2)}, u32[]{:S(2)}) %collective-permute-start.6) | collective-permute-done | bytes 4128 | tf_op jit(solution)/shard_map/ppermute | solution.py:611
  50.7 0.5 slice.27
  (6 shorter events, 0.0 us)
Async XLA Ops:
  1.6 15.7 %collective-permute-start = (f32[16,256]{1,0:T(8,128)S(1)}, f32[16,256]{1,0:T(8,128)S(1)}, u32[]{:S(2)}, u32[]{:S(2)}) collective-permute-start(f32[16,256]{1,0:T(8,128)S(1)} %get-tuple-element.32), channel_id=1, source_target_pairs={{0,4},{4,8},{8,12},{12,16},{16,20},{20,24},{24,28},{1,5},{5,9},{9,... | collective-permute-start | bytes 49160 | tf_op jit(solution)/shard_map/ppermute | solution.py:637
  6.5 10.8 %collective-permute-start.1 = (f32[16,256]{1,0:T(8,128)S(1)}, f32[16,256]{1,0:T(8,128)S(1)}, u32[]{:S(2)}, u32[]{:S(2)}) collective-permute-start(f32[16,256]{1,0:T(8,128)S(1)} %get-tuple-element.33), channel_id=1, source_target_pairs={{4,0},{8,4},{12,8},{16,12},{20,16},{24,20},{28,24},{5,1},{9,5},{13... | collective-permute-start | bytes 49160 | tf_op jit(solution)/shard_map/ppermute | solution.py:638
  29.7 4.3 %collective-permute-start.2 = (f32[2,8,128]{2,1,0:T(8,128)S(1)}, f32[2,8,128]{2,1,0:T(8,128)S(1)}, u32[]{:S(2)}, u32[]{:S(2)}) collective-permute-start(f32[2,8,128]{2,1,0:T(8,128)S(1)} %get-tuple-element.42), channel_id=1, source_target_pairs={{0,4},{4,0},{8,12},{12,8},{16,20},{20,16},{24,28},{28,24},{1,5},{5... | collective-permute-start | bytes 24584 | tf_op jit(solution)/shard_map/ppermute | solution.py:611
  34.0 3.7 %collective-permute-start.3 = (f32[2,8,128]{2,1,0:T(8,128)S(1)}, f32[2,8,128]{2,1,0:T(8,128)S(1)}, u32[]{:S(2)}, u32[]{:S(2)}) collective-permute-start(f32[2,8,128]{2,1,0:T(8,128)S(1)} %pad_maximum_fusion), channel_id=1, source_target_pairs={{0,8},{4,12},{8,0},{12,4},{16,24},{20,28},{24,16},{28,20},{1,9},{5... | collective-permute-start | bytes 24584 | tf_op jit(solution)/shard_map/ppermute | solution.py:611
  37.8 7.0 %collective-permute-start.4 = (f32[2,8,128]{2,1,0:T(8,128)S(1)}, f32[2,8,128]{2,1,0:T(8,128)S(1)}, u32[]{:S(2)}, u32[]{:S(2)}) collective-permute-start(f32[2,8,128]{2,1,0:T(8,128)S(1)} %pad_maximum_fusion.1.stat_ref), channel_id=1, source_target_pairs={{0,16},{4,20},{8,24},{12,28},{16,0},{20,4},{24,8},{28,12},{1,17},{... | collective-permute-start | bytes 24584 | tf_op jit(solution)/shard_map/ppermute | solution.py:611
  45.9 1.2 %collective-permute-start.5 = (f32[8,128]{1,0:T(8,128)S(1)}, f32[8,128]{1,0:T(8,128)S(1)}, u32[]{:S(2)}, u32[]{:S(2)}) collective-permute-start(f32[8,128]{1,0:T(8,128)S(1)} %get-tuple-element.45), channel_id=1, source_target_pairs={{0,1},{1,0},{2,3},{3,2},{4,5},{5,4},{6,7},{7,6},{8,9},{9,8},{10,11... | collective-permute-start | bytes 12296 | tf_op jit(solution)/shard_map/ppermute | solution.py:611
  47.1 3.6 %collective-permute-start.6 = (f32[8,128]{1,0:T(8,128)S(1)}, f32[8,128]{1,0:T(8,128)S(1)}, u32[]{:S(2)}, u32[]{:S(2)}) collective-permute-start(f32[8,128]{1,0:T(8,128)S(1)} %add.53), channel_id=1, source_target_pairs={{0,2},{1,3},{2,0},{3,1},{4,6},{5,7},{6,4},{7,5},{8,10},{9,11},{10,... | collective-permute-start | bytes 12296 | tf_op jit(solution)/shard_map/ppermute | solution.py:611
